TPU v7x, 32 devices: a whole 2x2x4 slice. The times are simulated.
32 devices in a mesh: expert: 2 (over x), dp: 16 (over z, y, core).
Axes of the slice: x: 2, y: 2, z: 4, core: 2. Of those that a mesh axis runs over, the one named last changes fastest.
Arguments:
- tokens: bfloat16 [384, 4096], P('expert'), may hold values from -6 to 6
- grad_out: bfloat16 [384, 4096], P('expert'), may hold values from -3 to 3
- gate_probs: bfloat16 [384, 2], P('expert'), may hold values from 0.19921875 to 1
- expert_ids: int32 [384, 2], P('expert'), may hold values from 0 to 3, all different within a row; in each aligned block of 192 rows (0 to 191, 192 to 383, ...) at most 144 rows name the same one
- capacity: int32 [4], replicated, may hold values from 72 to 144, as said below
- w_gate: bfloat16 [4096, 57344], P(None, 'dp'), may hold values from -0.09375 to 0.09375
- w_up: bfloat16 [4096, 57344], P(None, 'dp'), may hold values from -0.09375 to 0.09375
- w_down: bfloat16 [4096, 57344], P(None, 'dp'), may hold values from -0.046875 to 0.046875
Outputs:
- grad_tokens: bfloat16 [384, 4096], P('expert', 'dp')
- grad_probs: bfloat16 [384, 2], P('expert')
- grad_gate: bfloat16 [4096, 57344], P('expert', 'dp')
- grad_up: bfloat16 [4096, 57344], P('expert', 'dp')
- grad_down: bfloat16 [4096, 57344], P('expert', 'dp')
Inputs may be any that keep to these rules, and one draw needn't show every extreme that they name: `expert_ids`: the two experts of a token differ. Among the 192 tokens of one group no expert is named more than 144 times, a bound that some block reaches. Some expert has capacity 144 and another one 144 // 2.
All inputs are finite; a program needn't handle non-finite values.
Results may differ from a plain program's by a relative error of at most 0.013.
Values may be sent and summed in bfloat16 or wider, within the bound.
No kernel may reach another device: no remote copies, remote signals or barrier semaphores. Data moves between devices by JAX's collectives and lax.ppermute only.
A program may use at most 256 MiB of HBM per device.

v0:
```python
import jax
import jax.numpy as jnp
from jax import lax
from jax.sharding import PartitionSpec as P

EXPERTS = 4
CAP = 144


def routing_table(routes, capacity):
    flat_ids = routes.reshape(-1)
    expert_row = jnp.arange(EXPERTS, dtype=jnp.int32)
    onehot = (flat_ids[:, None] == expert_row[None, :]).astype(jnp.int32)
    earlier = jnp.cumsum(onehot, axis=0, dtype=jnp.int32) - onehot
    position = jnp.sum(earlier * onehot, axis=1, dtype=jnp.int32)
    limits = jnp.sum(onehot * capacity[None, :], axis=1, dtype=jnp.int32)
    target = flat_ids * CAP + position
    slot_rows = jnp.arange(EXPERTS * CAP, dtype=jnp.int32)
    chosen = (slot_rows[:, None] == target[None, :]) & (position < limits)[None, :]
    return chosen.astype(jnp.float32)


def per_device(tokens, grad_out, gate_probs, expert_ids, capacity, w_gate, w_up, w_down):
    groups = lax.axis_size("expert")
    model_width = w_gate.shape[0]
    token_count = tokens.shape[0]
    per_expert = lax.axis_size("dp") // EXPERTS
    owner = lax.axis_index("dp") // per_expert
    chosen = routing_table(expert_ids, capacity)
    own_table = lax.dynamic_slice_in_dim(chosen, owner * CAP, CAP, 0)
    pair_own = own_table.reshape(CAP, token_count, 2)
    merged = jnp.sum(pair_own, axis=2).astype(jnp.bfloat16)
    rows_x = jnp.dot(merged, tokens, preferred_element_type=jnp.float32).astype(jnp.bfloat16)
    rows_u = jnp.dot(merged, grad_out, preferred_element_type=jnp.float32).astype(jnp.bfloat16)
    rows_p = jnp.dot(
        own_table, gate_probs.reshape(-1).astype(jnp.float32), precision=lax.Precision.HIGHEST
    ).astype(jnp.bfloat16)
    weight_col = rows_p.astype(jnp.float32)[:, None]
    pre_gate = jnp.dot(rows_x, w_gate, preferred_element_type=jnp.float32)
    pre_up = jnp.dot(rows_x, w_up, preferred_element_type=jnp.float32)
    back_hidden = jnp.dot(rows_u, w_down, preferred_element_type=jnp.float32)
    sigmoid_gate = jax.nn.sigmoid(pre_gate)
    activated = pre_gate * sigmoid_gate
    hidden = (activated * pre_up).astype(jnp.bfloat16)
    prob_part = jnp.sum(hidden.astype(jnp.float32) * back_hidden, axis=1)
    scaled_back = weight_col * back_hidden
    d_gate = (scaled_back * pre_up * sigmoid_gate * (1.0 + pre_gate * (1.0 - sigmoid_gate))).astype(
        jnp.bfloat16
    )
    d_up = (scaled_back * activated).astype(jnp.bfloat16)
    scaled = (weight_col * rows_u.astype(jnp.float32)).astype(jnp.bfloat16)
    prob_tokens = jnp.einsum("rtk,r->tk", pair_own, prob_part, precision=lax.Precision.HIGHEST)
    prob_grad = lax.psum(prob_tokens, "dp").astype(jnp.bfloat16)
    contract_rows = (((0,), (0,)), ((), ()))
    contract_hidden = (((1,), (1,)), ((), ()))
    token_gate = lax.dot_general(
        merged, d_gate, contract_rows, preferred_element_type=jnp.float32
    ).astype(jnp.bfloat16)
    token_up = lax.dot_general(
        merged, d_up, contract_rows, preferred_element_type=jnp.float32
    ).astype(jnp.bfloat16)
    partial_rows = lax.dot_general(
        token_gate, w_gate, contract_hidden, preferred_element_type=jnp.float32
    )
    partial_rows = partial_rows + lax.dot_general(
        token_up, w_up, contract_hidden, preferred_element_type=jnp.float32
    )
    token_grad = lax.psum_scatter(partial_rows, "dp", scatter_dimension=1, tiled=True).astype(
        jnp.bfloat16
    )
    quarter = model_width // groups
    outgoing = jnp.stack([rows_x, scaled], axis=0).reshape(2, CAP, groups, quarter)
    arrived = lax.all_to_all(outgoing, "expert", split_axis=2, concat_axis=2, tiled=True)
    gate_all, up_all, hidden_all = (
        lax.all_gather(d_gate, "expert", axis=0, tiled=True),
        lax.all_gather(d_up, "expert", axis=0, tiled=True),
        lax.all_gather(hidden, "expert", axis=0, tiled=True),
    )
    gate_all = gate_all.reshape(groups, CAP, gate_all.shape[1])
    up_all = up_all.reshape(groups, CAP, up_all.shape[1])
    hidden_all = hidden_all.reshape(groups, CAP, hidden_all.shape[1])
    grad_gate = jnp.einsum(
        "cgq,gch->qh", arrived[0], gate_all, preferred_element_type=jnp.float32
    ).astype(jnp.bfloat16)
    grad_up = jnp.einsum(
        "cgq,gch->qh", arrived[0], up_all, preferred_element_type=jnp.float32
    ).astype(jnp.bfloat16)
    grad_down = jnp.einsum(
        "cgq,gch->qh", arrived[1], hidden_all, preferred_element_type=jnp.float32
    ).astype(jnp.bfloat16)
    return (token_grad, prob_grad, grad_gate, grad_up, grad_down)


def solution(mesh):
    return jax.shard_map(
        per_device,
        mesh=mesh,
        in_specs=(
            P("expert", None),
            P("expert", None),
            P("expert", None),
            P("expert", None),
            P(),
            P(None, "dp"),
            P(None, "dp"),
            P(None, "dp"),
        ),
        out_specs=(
            P("expert", "dp"),
            P("expert", None),
            P("expert", "dp"),
            P("expert", "dp"),
            P("expert", "dp"),
        ),
        check_vma=False,
    )
```

profile of v0, /device:TPU:0, one launch (start us, length us, event | category | flops | bytes accessed | tf_op | source)
XLA Modules:
  0.0 200.8 jit_solution(18374763205962185875)
XLA Ops:
  8.0 0.0 copy-start
  8.0 0.0 all-gather.6.cloned.1.call-start
  8.1 0.9 copy.20
  9.0 0.1 reshape.67
  9.1 0.1 eq.40
  9.3 0.8 copy.22
  10.1 0.2 reshape.75
  10.3 1.2 reduce-window.6
  11.5 0.2 slice_reduce_fusion
  11.7 0.2 reduce-window.9
  11.9 0.1 add_bitcast_fusion
  12.0 0.7 select_reduce_fusion.1
  12.7 0.2 fusion.2
  13.0 0.2 fusion.7
  13.2 0.2 reshape.69
  13.4 0.2 fusion.8
  13.6 0.6 reduce_sum.38
  14.1 1.9 convolution_convert_fusion.2
  16.0 11.7 %fusion.10 = f32[144,3584]{1,0:T(8,128)S(1)} fusion(bf16[144,4096]{1,0:T(8,128)(2,1)S(1)} %convolution_convert_fusion.2, bf16[4096,3584]{1,0:T(8,128)(2,1)} %param.13), kind=kOutput, calls=%fused_computation.38 | convolution fusion | flops 4227858432 | bytes 32604160 | tf_op jit(solution)/shard_map/dot_general | solution.py:39
  27.7 11.7 %fusion.9 = f32[144,3584]{1,0:T(8,128)S(1)} fusion(bf16[144,4096]{1,0:T(8,128)(2,1)S(1)} %convolution_convert_fusion.2, bf16[4096,3584]{1,0:T(8,128)(2,1)} %param.14), kind=kOutput, calls=%fused_computation.37 | convolution fusion | flops 4227858432 | bytes 32604160 | tf_op jit(solution)/shard_map/dot_general | solution.py:40
  39.4 1.9 multiply_convert_fusion
  41.4 16.5 %multiply_reduce_fusion = (f32[144]{0:T(256)S(1)}, bf16[144,3584]{1,0:T(8,128)(2,1)}, bf16[144,3584]{1,0:T(8,128)(2,1)}, bf16[144,3584]{1,0:T(8,128)(2,1)}) fusion(f32[144,3584]{1,0:T(8,128)S(1)} %fusion.9, f32[144,3584]{1,0:T(8,128)S(1)} %fusion.10, f32[144]{0:T(256)S(1)} %convert_convert_fusion, bf16[144,4096]{1,0:T(8,128)(2,1)} %get-tuple-element.14, ...), kind=kOutput, calls=%fused_computation.10 | convolution fusion | flops 4237664000 | bytes 37766272 | tf_op jit(solution)/shard_map/dot_general | solution.py:41
  57.8 0.0 all-gather.6.cloned.1.call-update
  57.9 0.0 all-gather.4.cloned.1.call-start
  57.9 0.7 all-gather.4.cloned.1.call-update
  58.6 0.0 copy-start.2
  58.6 1.9 stack.9
  60.5 2.7 %copy.23 = bf16[1,144,2,2048]{3,1,0,2:T(8,128)(2,1)} copy(bf16[1,144,2,2048]{3,2,1,0:T(2,128)(2,1)} %stack.9) | data formatting | bytes 2359296 | tf_op jit(solution)/shard_map/stack | solution.py:72
  63.2 0.9 stack.10
  64.1 0.4 copy.24
  64.5 0.8 copy-done.3
  65.4 1.6 pad_maximum_fusion
  67.0 5.2 %all-to-all-start = ((bf16[2,144,2,2048]{3,1,0,2:T(8,128)(2,1)}), bf16[2,144,2,2048]{3,1,0,2:T(8,128)(2,1)}, u32[]{:S(2)}, u32[]{:S(2)}) async-start(bf16[2,144,2,2048]{3,1,0,2:T(8,128)(2,1)} %pad_maximum_fusion), calls=%async_computation.1 | async-start | bytes 4718592 | tf_op jit(solution)/shard_map/all_to_all | solution.py:73
  72.2 0.0 all-gather.8.cloned.1.call-start
  72.2 0.7 all-gather.8.cloned.1.call-update
  72.9 0.0 reduce-scatter.2.cloned.1.call-start
  73.0 16.0 %fusion.1 = f32[192,4096]{1,0:T(8,128)} fusion(bf16[4096,3584]{1,0:T(8,128)(2,1)} %param.13, bf16[144,192]{0,1:T(8,128)(2,1)S(1)} %reduce_sum.38, bf16[144,3584]{1,0:T(8,128)(2,1)S(1)} %copy-done.4), kind=kOutput, calls=%fused_computation.16 | convolution fusion | flops 5836013568 | bytes 33593344 | tf_op jit(solution)/shard_map/dot_general | solution.py:62
  89.0 16.5 %convolution_add_fusion = f32[192,4096]{1,0:T(8,128)} fusion(f32[192,4096]{1,0:T(8,128)} %fusion.1, bf16[4096,3584]{1,0:T(8,128)(2,1)} %param.14, bf16[144,192]{0,1:T(8,128)(2,1)S(1)} %reduce_sum.38, bf16[144,3584]{1,0:T(8,128)(2,1)S(1)} %copy-done.5), kind=kOutput, calls=%fused_computation.3 | convolution fusion | flops 5836800000 | bytes 36739072 | tf_op jit(solution)/shard_map/dot_general | solution.py:65
  105.5 0.0 reduce-scatter.2.cloned.1.call-update
  105.5 0.1 reshape.71
  105.6 0.4 select_reduce_fusion
  106.0 0.1 copy.30
  106.1 35.5 %psum.7 = bf16[192,2]{0,1:T(2,128)(2,1)} all-reduce(f32[192,2]{0,1:T(2,128)S(1)} %copy.30), channel_id=1, replica_groups=mesh['expert'=2,'dp'=16] {'dp'}, use_global_device_ids=true, to_apply=%region_7.8 | all-reduce | flops 384 | bytes 2304 | tf_op jit(solution)/shard_map/psum | solution.py:53
  141.6 13.0 %bitcast_convert_fusion.1 = bf16[2048,3584]{1,0:T(8,128)(2,1)} fusion(bf16[2,144,3584]{2,1,0:T(8,128)(2,1)} %bitcast.67, bf16[2,144,2,2048]{3,1,0,2:T(8,128)(2,1)} %all-to-all-done), kind=kOutput, calls=%fused_computation.1 | convolution fusion | flops 4235198464 | bytes 17924096 | tf_op jit(solution)/shard_map/cgq,gch->qh/dot_general | solution.py:85
  154.6 13.2 %bitcast_convert_fusion.2 = bf16[2048,3584]{1,0:T(8,128)(2,1)} fusion(bf16[2,144,3584]{2,1,0:T(8,128)(2,1)} %bitcast.68, bf16[2,144,2,2048]{3,1,0,2:T(8,128)(2,1)} %all-to-all-done), kind=kOutput, calls=%fused_computation.2 | convolution fusion | flops 4235198464 | bytes 17924096 | tf_op jit(solution)/shard_map/cgq,gch->qh/dot_general | solution.py:82
  167.8 11.3 %all-gather.8.cloned.1.call-done = bf16[288,3584]{1,0:T(8,128)(2,1)} async-done(((bf16[144,3584]{1,0:T(8,128)(2,1)}), bf16[288,3584]{1,0:T(8,128)(2,1)}) %all-gather.8.cloned.1.call-update) | async-done | bytes 2064400 | tf_op jit(solution)/shard_map/all_gather | solution.py:77
  179.1 13.0 %bitcast_convert_fusion = bf16[2048,3584]{1,0:T(8,128)(2,1)} fusion(bf16[2,144,3584]{2,1,0:T(8,128)(2,1)} %bitcast.69, bf16[2,144,2,2048]{3,1,0,2:T(8,128)(2,1)} %all-to-all-done), kind=kOutput, calls=%fused_computation | convolution fusion | flops 4235198464 | bytes 17924096 | tf_op jit(solution)/shard_map/cgq,gch->qh/dot_general | solution.py:88
  192.1 1.6 convert_element_type.77
  (17 shorter events, 0.0 us)
Async XLA Ops:
  8.0 31.4 %copy-start = (bf16[192,4096]{1,0:T(8,128)(2,1)S(1)}, bf16[192,4096]{1,0:T(8,128)(2,1)}, u32[]{:S(2)}) copy-start(bf16[192,4096]{1,0:T(8,128)(2,1)} %param.9) | copy-start | bytes 4718596
  8.0 133.6 %all-gather.6.cloned.1.call-start = ((), (), s32[]{:S(2)}) async-start(), calls=%async_computation.4 | async-start | bytes 3096576 | tf_op jit(solution)/shard_map/all_gather | solution.py:76
  57.9 96.7 %all-gather.4.cloned.1.call-start = ((), (), s32[]{:S(2)}) async-start(), calls=%async_computation.3 | async-start | bytes 3096576 | tf_op jit(solution)/shard_map/all_gather | solution.py:75
  58.6 4.6 %copy-start.2 = (bf16[144,4096]{1,0:T(8,128)(2,1)S(1)}, bf16[144,4096]{1,0:T(8,128)(2,1)}, u32[]{:S(2)}) copy-start(bf16[144,4096]{1,0:T(8,128)(2,1)} %get-tuple-element.13) | copy-start | bytes 3538948
  64.1 1.3 copy-start.3
  67.0 6.0 %copy-start.4 = (bf16[144,3584]{1,0:T(8,128)(2,1)S(1)}, bf16[144,3584]{1,0:T(8,128)(2,1)}, u32[]{:S(2)}) copy-start(bf16[144,3584]{1,0:T(8,128)(2,1)} %get-tuple-element.11) | copy-start | bytes 3096580
  67.0 74.6 %all-to-all-start = ((bf16[2,144,2,2048]{3,1,0,2:T(8,128)(2,1)}), bf16[2,144,2,2048]{3,1,0,2:T(8,128)(2,1)}, u32[]{:S(2)}, u32[]{:S(2)}) async-start(bf16[2,144,2,2048]{3,1,0,2:T(8,128)(2,1)} %pad_maximum_fusion), calls=%async_computation.1 | async-start | bytes 4718592 | tf_op jit(solution)/shard_map/all_to_all | solution.py:73
  72.2 106.9 %all-gather.8.cloned.1.call-start = ((), (), s32[]{:S(2)}) async-start(), calls=%async_computation.5 | async-start | bytes 3096576 | tf_op jit(solution)/shard_map/all_gather | solution.py:77
  72.9 16.1 %copy-start.5 = (bf16[144,3584]{1,0:T(8,128)(2,1)S(1)}, bf16[144,3584]{1,0:T(8,128)(2,1)}, u32[]{:S(2)}) copy-start(bf16[144,3584]{1,0:T(8,128)(2,1)} %get-tuple-element.12) | copy-start | bytes 3096580
  72.9 119.2 %reduce-scatter.2.cloned.1.call-start = ((), (), s32[]{:S(2)}) async-start(), calls=%async_computation.2 | async-start | bytes 3342336 | tf_op jit(solution)/shard_map/reduce_scatter | solution.py:68
  179.1 14.6 %copy-start.1 = (bf16[192,4096]{1,0:T(8,128)(2,1)S(1)}, bf16[192,4096]{1,0:T(8,128)(2,1)}, u32[]{:S(2)}) copy-start(bf16[192,4096]{1,0:T(8,128)(2,1)} %param.9) | copy-start | bytes 4718596
Sparse Core Ops, SparseCore 0:
  58.0 52.6 all-gather.5
  112.2 32.4 all-gather.3
  146.3 32.7 all-gather.7
Sparse Core Ops, SparseCore 1:
  105.6 69.3 reduce-scatter.1
where the time goes:
time: 201 us
  matrix products  115 us (57%)
  blocking collectives  35.5 us (18%)
  between operations  15.4 us (8%)
  waiting for transfers between devices  12.8 us (6%)
  local copies, waits for them, and re-layouts  9.59 us (5%)
  other arithmetic  6.77 us (3%)
  starting transfers between devices  5.33 us (3%)
    psum x1, blocking collectives, per_device(): prob_grad = lax.psum(prob_tokens, 'dp').astype(jnp.bfloat16)  35.5 us
    dot_general x1, matrix products, per_device(): lax.dot_general(token_up, w_up, contract_hidden, preferred_element_type=j...  16.5 us
    dot_general x1, matrix products, per_device(): back_hidden = jnp.dot(rows_u, w_down, preferred_element_type=jnp.float32)  16.5 us
    dot_general x1, matrix products, per_device(): lax.dot_general(token_gate, w_gate, contract_hidden, preferred_element_ty...  16 us
    dot_general x1, matrix products, per_device(): jnp.einsum('cgq,gch->qh', arrived[0], gate_all, preferred_element_type=jn...  13.2 us
    dot_general x1, matrix products, per_device(): jnp.einsum('cgq,gch->qh', arrived[0], up_all, preferred_element_type=jnp....  13 us
    dot_general x1, matrix products, per_device(): jnp.einsum('cgq,gch->qh', arrived[1], hidden_all, preferred_element_type=...  13 us
    dot_general x1, matrix products, per_device(): pre_up = jnp.dot(rows_x, w_up, preferred_element_type=jnp.float32)  11.7 us
  transfers between devices with their start and end apart: 5, of which 1 were waited for; matrix products, arithmetic and copies ran while one was open for 40% of the time, Pallas kernels for 0%

commit v1 on v0

v1 whole, which is shorter than its diff:
```python
import functools

import jax
import jax.numpy as jnp
from jax import lax
from jax.experimental import pallas as pl
from jax.experimental.pallas import tpu as pltpu
from jax.sharding import PartitionSpec as P

EXPERTS = 4
CAP = 144
SHORT = 256
EXTRA = 16
BF = jnp.bfloat16
F32 = jnp.float32
VMEM_LIMIT = 60 * 1024 * 1024

FIRST = (((0,), (0,)), ((), ()))
LAST = (((1,), (1,)), ((), ()))


def dot(a, b):
    return jnp.dot(a, b, preferred_element_type=F32)


def dotg(a, b, dims):
    return lax.dot_general(a, b, dims, preferred_element_type=F32)


def whole(shape):
    return pl.BlockSpec(shape, lambda *_: (0,) * len(shape), pipeline_mode=pl.Buffered(1))


def params():
    return pltpu.CompilerParams(vmem_limit_bytes=VMEM_LIMIT)


def whole_smem():
    return pl.BlockSpec(memory_space=pltpu.SMEM)


def in_place():
    return pl.BlockSpec(memory_space=pl.ANY)


def slot_table(routes, owner, limit, backwards):
    count = routes.shape[1]
    hit = (routes[:2] == owner.astype(F32)).astype(F32)
    named = jnp.sum(hit, axis=0, keepdims=True)
    weight = jnp.sum(hit * routes[2:4], axis=0, keepdims=True)
    row = lax.broadcasted_iota(jnp.int32, (count, count), 0)
    col = lax.broadcasted_iota(jnp.int32, (count, count), 1)
    earlier = (row < col).astype(F32).astype(BF)
    wide = jnp.broadcast_to(named, (16, count)).astype(BF)
    rank = dot(wide, earlier)[:1].astype(jnp.int32)
    kept = (named > 0) & (rank < limit)
    slot = lax.broadcasted_iota(jnp.int32, (CAP, count), 0)
    if backwards:
        slot = CAP - 1 - slot
    table = ((slot == rank) & kept).astype(F32)
    return table, jnp.sum(table * weight, axis=1, keepdims=True)


class Stream:
    def __init__(self, sources, slots, sems, block):
        self.sources, self.slots, self.sems, self.block = sources, slots, sems, block
        self.steps = sources[0].shape[1] // block

    def copy(self, i, step):
        source = self.sources[i]
        if self.steps > 1:
            source = source.at[:, pl.ds(pl.multiple_of(step * self.block, self.block), self.block)]
        slot = lax.rem(step, 2)
        return pltpu.make_async_copy(source, self.slots[i].at[slot], self.sems.at[i, slot])

    def first(self):
        for i in range(len(self.sources)):
            self.copy(i, 0).start()

    def ahead(self, step):
        @pl.when(step + 1 < self.steps)
        def _():
            for i in range(len(self.sources)):
                self.copy(i, step + 1).start()

    def wait(self, i, step):
        self.copy(i, step).wait()
        return self.slots[i].at[lax.rem(step, 2)]


def derivatives(x_ref, u_ref, p, stream, step):
    x = x_ref[...]
    wg = stream.wait(0, step)
    pre_gate = dot(x, wg[...])
    wu = stream.wait(1, step)
    pre_up = dot(x, wu[...])
    wd = stream.wait(2, step)
    back = dot(u_ref[...], wd[...])
    s = jax.nn.sigmoid(pre_gate)
    activated = pre_gate * s
    hidden = (activated * pre_up).astype(BF)
    scaled_back = p * back
    d_gate = (scaled_back * pre_up * s * (1.0 + pre_gate * (1.0 - s))).astype(BF)
    d_up = (scaled_back * activated).astype(BF)
    return d_gate, d_up, hidden, back, wg, wu


def pieces_of(total, size):
    return [(a, min(size, total - a)) for a in range(0, total, size)]


def own_body(packed, place_ref, cap_ref, routes_ref, tok_hbm, out_hbm, wg_hbm, wu_hbm, wd_hbm,
             dg_ref, du_ref, h_ref, part_ref, prob_ref, xq_ref, sq_ref, filled_ref,
             tok_ref, out_ref, x_ref, u_ref, p_ref, table_ref, acc_ref, wg_ref, wu_ref, wd_ref, sems, row_sems):
    step = pl.program_id(0)
    width, block = wg_ref.shape[1:]
    quarter = xq_ref.shape[1]
    stream = Stream((wg_hbm, wu_hbm, wd_hbm), (wg_ref, wu_ref, wd_ref), sems, block)
    owner, group = place_ref[0], place_ref[2]

    @pl.when(step == 0)
    def _():
        rows = [pltpu.make_async_copy(tok_hbm, tok_ref, row_sems.at[0]),
                pltpu.make_async_copy(out_hbm, out_ref, row_sems.at[1])]
        for copy in rows:
            copy.start()
        stream.first()
        table, p = slot_table(routes_ref[...].astype(F32), owner, cap_ref[owner], False)
        table_ref[...] = table.astype(BF)
        p_ref[...] = p
        filled_ref[...] = jnp.sum(table, axis=1, keepdims=True)
        acc_ref[...] = jnp.zeros_like(acc_ref)
        prob_ref[...] = jnp.zeros_like(prob_ref)
        rows[0].wait()
        x_ref[...] = dot(table_ref[...], tok_ref[...]).astype(BF)
        rows[1].wait()
        u_ref[...] = dot(table_ref[...], out_ref[...]).astype(BF)
        at = pl.ds(pl.multiple_of(group * quarter, quarter), quarter)
        xq_ref[...] = x_ref[:, at]
        sq_ref[...] = (p * u_ref[:, at].astype(F32)).astype(BF)

    stream.ahead(step)
    d_gate, d_up, hidden, back, wg, wu = derivatives(x_ref, u_ref, p_ref[...], stream, step)
    dg_ref[...] = d_gate
    du_ref[...] = d_up
    h_ref[...] = hidden
    prob_ref[...] += jnp.sum(hidden.astype(F32) * back, axis=1, keepdims=True)
    gate_t = d_gate.T
    up_t = d_up.T
    for a, n in pieces_of(width, 512):
        at = slice(a, a + n)
        acc_ref[at, :] += dot(wg[at, :], gate_t) + dot(wu[at, :], up_t)

    @pl.when(step == pl.num_programs(0) - 1)
    def _():
        table = table_ref[...]
        count = table.shape[1]
        shares, _, fw = part_ref.shape
        by_slot = (((0,), (1,)), ((), ()))
        for j in range(shares):
            part_ref[j, :count, :] = dotg(table, acc_ref[j * fw:(j + 1) * fw, :].astype(BF), by_slot).astype(BF)
        if packed:
            total = prob_ref[...]
            high = total.astype(BF).astype(F32)
            lane = lax.broadcasted_iota(jnp.int32, (CAP, 128), 1)
            both = jnp.where(lane == 0, high, jnp.where(lane == 1, total - high, 0.0)).astype(BF)
            by_token = dotg(both, table, FIRST)[:EXTRA].astype(BF)
            for j in range(shares):
                part_ref[j, count:, :] = jnp.zeros((EXTRA, fw), BF)
                part_ref[j, count:, :count] = by_token


def weight_slots(width, block):
    return [pltpu.VMEM((2, width, block), BF)] * 3 + [pltpu.SemaphoreType.DMA((3, 2))]


def own_group(place, capacity, routes, tokens, grad_out, wg, wu, wd, shares, groups, packed, block):
    count, width = tokens.shape
    hidden = wg.shape[1]
    tall = count + (EXTRA if packed else 0)
    fw = width // shares
    quarter = width // groups
    act = pl.BlockSpec((CAP, block), lambda j: (0, j))
    acts = jax.ShapeDtypeStruct((CAP, hidden), BF)
    column = jax.ShapeDtypeStruct((CAP, 1), F32)
    share = jax.ShapeDtypeStruct((CAP, quarter), BF)
    part = jax.ShapeDtypeStruct((shares, tall, fw), BF)
    rows = pltpu.VMEM((CAP, width), BF)
    tall_rows = pltpu.VMEM((count, width), BF)
    return pl.pallas_call(
        functools.partial(own_body, packed),
        grid=(hidden // block,),
        in_specs=[whole_smem(), whole_smem(), whole(routes.shape)] + [in_place()] * 5,
        out_specs=[act, act, act, whole(part.shape), whole(column.shape), whole(share.shape), whole(share.shape),
                   whole(column.shape)],
        out_shape=[acts, acts, acts, part, column, share, share, column],
        scratch_shapes=[tall_rows, tall_rows, rows, rows, pltpu.VMEM((CAP, 1), F32), pltpu.VMEM((CAP, count), BF),
                        pltpu.VMEM((width, CAP), F32)] + weight_slots(width, block) + [pltpu.SemaphoreType.DMA((2,))],
        compiler_params=params(),
        cost_estimate=pl.CostEstimate(
            flops=10 * CAP * width * hidden, bytes_accessed=6 * width * hidden, transcendentals=CAP * hidden),
        name="own_group",
    )(place, capacity, routes, tokens, grad_out, wg, wu, wd)


def weights_body(groups, place_ref, cap_ref, xq_ref, sq_ref, filled_ref, one_hbm, two_hbm, dg_ref, du_ref, h_ref,
                 wg_hbm, wu_hbm, wd_hbm, gg_ref, gu_ref, gd_ref,
                 one_ref, two_ref, xo_ref, uo_ref, po_ref, xs_ref, ss_ref, short_ref, wg_ref, wu_ref, wd_ref, sems, row_sems):
    step = pl.program_id(0)
    owner, parity, group = place_ref[0], place_ref[1], place_ref[2]
    quarter = xs_ref.shape[1]
    others = xo_ref.shape[0]
    count = one_ref.shape[1] - EXTRA
    lead = SHORT - CAP
    shared = CAP - lead
    stream = Stream((wg_hbm, wu_hbm, wd_hbm), (wg_ref, wu_ref, wd_ref), sems, wg_ref.shape[2])

    def joined(mine, other):
        return jnp.concatenate([mine, other], axis=0)

    def merged(mine, other):
        return jnp.concatenate([mine[:lead], mine[lead:] + other[:shared], other[shared:]], axis=0)

    @pl.when(step == 0)
    def _():
        rows = [pltpu.make_async_copy(one_hbm, one_ref, row_sems.at[0]),
                pltpu.make_async_copy(two_hbm, two_ref, row_sems.at[1])]
        for copy in rows:
            copy.start()
        stream.first()
        for copy in rows:
            copy.wait()
        filled = jnp.sum(filled_ref[...])
        for g in range(groups - 1):
            at = slice(g * CAP, (g + 1) * CAP)
            routes = one_ref[g, count:count + 8, :count].astype(F32)
            table, p = slot_table(routes, owner, cap_ref[owner], groups == 2)
            filled += jnp.sum(table)
            po_ref[at, :] = p
            table = table.astype(BF)
            from_one = dot(table, one_ref[g, :count, :]).astype(BF)
            from_two = dot(table, two_ref[g, :count, :]).astype(BF)

            @pl.when(parity == 0)
            def _():
                xo_ref[at, :] = from_one
                uo_ref[at, :] = from_two

            @pl.when(parity == 1)
            def _():
                xo_ref[at, :] = from_two
                uo_ref[at, :] = from_one

        fits = filled <= SHORT if groups == 2 else jnp.bool_(False)
        short_ref[0] = fits.astype(jnp.int32)
        part = pl.ds(pl.multiple_of(group * quarter, quarter), quarter)
        mine, scaled = xq_ref[...], sq_ref[...]
        other = xo_ref[:, part]
        scaled_other = (po_ref[...] * uo_ref[:, part].astype(F32)).astype(BF)
        if groups == 2:
            @pl.when(fits)
            def _():
                xs_ref[:SHORT, :] = merged(mine, other)
                ss_ref[:SHORT, :] = merged(scaled, scaled_other)

        @pl.when(jnp.logical_not(fits))
        def _():
            xs_ref[...] = joined(mine, other)
            ss_ref[...] = joined(scaled, scaled_other)

    stream.ahead(step)
    d_gate, d_up, hidden, _, _, _ = derivatives(xo_ref, uo_ref, po_ref[...], stream, step)

    def grads(join, rows):
        xs = xs_ref[:rows, :]
        gg_ref[...] = dotg(xs, join(dg_ref[...], d_gate), FIRST).astype(BF)
        gu_ref[...] = dotg(xs, join(du_ref[...], d_up), FIRST).astype(BF)
        gd_ref[...] = dotg(ss_ref[:rows, :], join(h_ref[...], hidden), FIRST).astype(BF)

    if groups == 2:
        @pl.when(short_ref[0] == 1)
        def _():
            grads(merged, SHORT)

    @pl.when(short_ref[0] == 0)
    def _():
        grads(joined, CAP + others)


def weight_grads(place, capacity, xq, sq, filled, one, two, dg, du, h, wg, wu, wd, groups, block):
    width, hidden = wg.shape
    others = (groups - 1) * CAP
    quarter = width // groups
    act = pl.BlockSpec((CAP, block), lambda j: (0, j))
    grad = pl.BlockSpec((quarter, block), lambda j: (0, j))
    arrived = pltpu.VMEM(one.shape, BF)
    rows = pltpu.VMEM((others, width), BF)
    share = pltpu.VMEM((CAP + others, quarter), BF)
    return pl.pallas_call(
        functools.partial(weights_body, groups),
        grid=(hidden // block,),
        in_specs=[whole_smem(), whole_smem(), whole(xq.shape), whole(sq.shape), whole(filled.shape), in_place(), in_place(),
                  act, act, act, in_place(), in_place(), in_place()],
        out_specs=[grad] * 3,
        out_shape=[jax.ShapeDtypeStruct((quarter, hidden), BF)] * 3,
        scratch_shapes=[arrived, arrived, rows, rows, pltpu.VMEM((others, 1), F32), share, share,
                        pltpu.SMEM((1,), jnp.int32)] + weight_slots(width, block) + [pltpu.SemaphoreType.DMA((2,))],
        compiler_params=params(),
        cost_estimate=pl.CostEstimate(
            flops=6 * others * width * hidden + 6 * (CAP + others) * quarter * hidden,
            bytes_accessed=6 * width * hidden + 6 * quarter * hidden, transcendentals=others * hidden),
        name="weight_grads",
    )(place, capacity, xq, sq, filled, one, two, dg, du, h, wg, wu, wd)


def block_of(hidden, largest):
    for size in (512, 256, 128):
        if size <= largest and hidden % size == 0:
            return size
    return hidden


def per_device(tokens, grad_out, gate_probs, expert_ids, capacity, w_gate, w_up, w_down):
    groups = lax.axis_size("expert")
    shares = lax.axis_size("dp")
    count, width = tokens.shape
    hidden = w_gate.shape[1]
    per_expert = shares // EXPERTS
    index = lax.axis_index("dp")
    owner = index // per_expert
    parity = index % 2
    place = jnp.stack([owner, parity, lax.axis_index("expert")]).astype(jnp.int32)
    packed = width // shares >= count

    routes = jnp.concatenate([expert_ids.T.astype(BF), gate_probs.T, jnp.zeros((EXTRA - 4, count), BF)], axis=0)
    send = jnp.concatenate(
        [jnp.where(parity == 0, tokens, grad_out), jnp.pad(routes, ((0, 0), (0, width - count)))], axis=0)
    arounds = [[(i, (i + shift) % groups) for i in range(groups)] for shift in range(1, groups)]
    one = [lax.ppermute(send, "expert", around) for around in arounds]

    dg, du, h, part, prob, xq, sq, filled = own_group(
        place, capacity, routes, tokens, grad_out, w_gate, w_up, w_down, shares, groups, packed, block_of(hidden, 512))

    one, part = lax.optimization_barrier((one, part))
    swap = [(i, i ^ 1) for i in range(shares)]
    two = [lax.ppermute(rows, "dp", swap) for rows in one]
    arrived = lax.all_to_all(part, "dp", split_axis=0, concat_axis=0, tiled=True)

    def stacked(parts):
        return parts[0][None] if len(parts) == 1 else jnp.stack(parts)

    grad_gate, grad_up, grad_down = weight_grads(
        place, capacity, xq, sq, filled, stacked(one), stacked(two), dg, du, h, w_gate, w_up, w_down, groups,
        block_of(hidden, 512))

    token_grad = jnp.sum(arrived[:, :count].astype(F32), axis=0).astype(BF)
    if packed:
        ends = arrived[:, count:count + 2, :count].astype(F32)
        by_expert = jnp.sum(ends.reshape(EXPERTS, per_expert * 2, count), axis=1)
    else:
        table, _ = slot_table(routes.astype(F32), owner, capacity[owner], False)
        mine = jnp.sum(table * prob, axis=0)
        one_hot = (jnp.arange(EXPERTS) == owner).astype(F32)
        by_expert = lax.psum(one_hot[:, None] * mine[None, :], "dp")
    match = expert_ids[:, :, None] == jnp.arange(EXPERTS, dtype=jnp.int32)
    prob_grad = jnp.sum(jnp.where(match, by_expert.T[:, None, :], 0.0), axis=2).astype(BF)
    return (token_grad, prob_grad, grad_gate, grad_up, grad_down)


def solution(mesh):
    return jax.shard_map(
        per_device,
        mesh=mesh,
        in_specs=(
            P("expert", None),
            P("expert", None),
            P("expert", None),
            P("expert", None),
            P(),
            P(None, "dp"),
            P(None, "dp"),
            P(None, "dp"),
        ),
        out_specs=(
            P("expert", "dp"),
            P("expert", None),
            P("expert", "dp"),
            P("expert", "dp"),
            P("expert", "dp"),
        ),
        check_vma=False,
    )
```

time: 201 us -> 112 us (0.56)
  matrix products: 115 us -> 0 us
  Pallas kernels: 0 us -> 94.8 us
  blocking collectives: 35.5 us -> 0 us
  between operations: 15.4 us -> 0.76 us
  waiting for transfers between devices: 12.8 us -> 0.01 us
  local copies, waits for them, and re-layouts: 9.59 us -> 1.19 us
  starting transfers between devices: 5.33 us -> 9.02 us
    dot_general x11 -> x0, matrix products: 115 us -> none  [the longest x1 16.5 us: per_device(): lax.dot_general(token_up, w_up, contract_hidden, preferred_element_type=j...]
    pallas_call x0 -> x2, Pallas kernels: none -> 94.8 us  [the longest x1 50.8 us: weight_grads(): pl.pallas_call(functools.partial(weights_body, groups), grid=(hidden // b...]
    psum x1 -> x0, blocking collectives: 35.5 us -> none  [per_device(): prob_grad = lax.psum(prob_tokens, 'dp').astype(jnp.bfloat16)]
    all_gather x3 -> x0, waiting for transfers between devices: 11.3 us -> none  [the longest x1 11.3 us: per_device(): lax.all_gather(hidden, 'expert', axis=0, tiled=True)]
    another operation x4 -> x0, local copies, waits for them, and re-layouts: 5.89 us -> none  [per_device(): jnp.stack([rows_x, scaled], axis=0).reshape(2, CAP, groups, quarter)]
    ppermute x0 -> x2, starting transfers between devices: none -> 3.08 us  [the longest x1 3 us: per_device(): one = [lax.ppermute(send, 'expert', around) for around in arounds]]
    another operation x3 -> x1, other arithmetic: 3.02 us -> 0.65 us  [per_device(): jnp.stack([owner, parity, lax.axis_index('expert')]).astype(jnp.int32)]
  transfers between devices with their start and end apart: 5 -> 3, of which waited for: 1 -> 0; matrix products, arithmetic and copies ran while one was open for 40% -> 1% of each run, Pallas kernels for 0% -> 85%
where the time goes in v1:
time: 112 us; the launch traced here: 111 us
  Pallas kernels  94.8 us (85%)
  starting transfers between devices  9.02 us (8%)
  other arithmetic  5.41 us (5%)
  local copies, waits for them, and re-layouts  1.19 us (1%)
    pallas_call x1, Pallas kernels, weight_grads(): pl.pallas_call(functools.partial(weights_body, groups), grid=(hidden // b...  50.8 us
    pallas_call x1, Pallas kernels, own_group(): pl.pallas_call(functools.partial(own_body, packed), grid=(hidden // block...  43.9 us
    all_to_all x1, starting transfers between devices, per_device(): lax.all_to_all(part, 'dp', split_axis=0, concat_axis=0, tiled=True)  5.95 us
    ppermute x1, starting transfers between devices, per_device(): one = [lax.ppermute(send, 'expert', around) for around in arounds]  3 us
  transfers between devices with their start and end apart: 3, of which 0 were waited for; matrix products, arithmetic and copies ran while one was open for 1% of the time, Pallas kernels for 85%

profile of v1, /device:TPU:0, one launch (start us, length us, event | category | flops | bytes accessed | tf_op | source)
XLA Modules:
  0.0 111.2 jit_solution(5191390858196924105)
XLA Ops:
  0.6 0.7 convert_bitcast_fusion
  1.3 0.1 pad.12.clone
  1.4 0.8 maximum_maximum_fusion.routes_ref
  2.2 0.0 copy-start.1
  2.2 1.6 %broadcast_select_fusion = bf16[192,4096]{1,0:T(8,128)(2,1)S(1)} fusion(bf16[192,4096]{1,0:T(8,128)(2,1)} %tok_hbm.1, bf16[192,4096]{1,0:T(8,128)(2,1)} %out_hbm.1, pred[]{:T(512)S(6)} %eq.18), kind=kLoop, calls=%fused_computation.4 | loop fusion | flops 786432 | bytes 4718593 | tf_op jit(solution)/shard_map/jit(_where)/select_n | solution.py:337
  3.8 0.0 copy-done.1
  3.8 0.2 fusion.1
  4.0 3.0 %collective-permute-start = (bf16[208,4096]{1,0:T(8,128)(2,1)S(1)}, bf16[208,4096]{1,0:T(8,128)(2,1)S(1)}, u32[]{:S(2)}, u32[]{:S(2)}) collective-permute-start(bf16[208,4096]{1,0:T(8,128)(2,1)S(1)} %fusion.1), channel_id=1, source_target_pairs={{0,16},{16,0},{1,17},{17,1},{2,18},{18,2},{3,19},{19,3},{4,20},{20... | collective-permute-start | bytes 5111816 | tf_op jit(solution)/shard_map/ppermute | solution.py:339
  7.0 0.7 pad_add_fusion.place_ref
  7.7 43.9 %own_group.1 = (bf16[144,3584]{1,0:T(8,128)(2,1)}, bf16[144,3584]{1,0:T(8,128)(2,1)}, bf16[144,3584]{1,0:T(8,128)(2,1)}, bf16[16,208,256]{2,1,0:T(8,128)(2,1)}, ...) custom-call(s32[3]{0:T(128)} %pad_add_fusion.place_ref, ...), custom_call_target="tpu_custom_call" | custom-call | flops 21139292160 | bytes 88080384 | tf_op jit(solution)/shard_map/own_group/pallas_call | solution.py:190
  51.6 0.0 collective-permute-done
  51.6 0.0 copy-start
  51.6 0.1 collective-permute-start.1
  51.7 1.1 copy-done
  52.8 5.9 %all-to-all-start = ((bf16[16,208,256]{2,1,0:T(8,128)(2,1)}), bf16[16,208,256]{2,1,0:T(8,128)(2,1)S(1)}, u32[]{:S(2)}, u32[]{:S(2)}) async-start(bf16[16,208,256]{2,1,0:T(8,128)(2,1)} %get-tuple-element.18), calls=%async_computation | async-start | bytes 3407872 | tf_op jit(solution)/shard_map/all_to_all | solution.py:347
  58.7 0.0 collective-permute-done.1
  58.8 0.0 copy-start.2
  58.8 50.8 %weight_grads.1 = (bf16[2048,3584]{1,0:T(8,128)(2,1)}, bf16[2048,3584]{1,0:T(8,128)(2,1)}, bf16[2048,3584]{1,0:T(8,128)(2,1)}) custom-call(s32[3]{0:T(128)} %pad_add_fusion.place_ref, s32[4]{0:T(128)} %cap_ref.3, bf16[144,2048]{1,0:T(8,128)(2,1)} %get-tuple-element.19.xq_ref, bf16[144,2048]{1,0:T(8,128)(2,1)} %get-tuple-element.20.sq_ref, ...), custom_call_target="tpu_custom_call" | custom-call | flops 25367150592 | bytes 132120576 | tf_op jit(solution)/shard_map/weight_grads/pallas_call | solution.py:299
  109.6 0.0 all-to-all-done
  109.7 0.0 copy-done.2
  109.7 0.6 select_reduce_fusion
  110.3 0.9 slice_reduce_fusion
  (4 shorter events, 0.1 us)
Async XLA Ops:
  2.2 1.6 %copy-start.1 = (bf16[16,192]{1,0:T(8,128)(2,1)}, bf16[16,192]{1,0:T(8,128)(2,1)S(1)}, u32[]{:S(2)}) copy-start(bf16[16,192]{1,0:T(8,128)(2,1)S(1)} %maximum_maximum_fusion.routes_ref) | copy-start | bytes 18436
  4.0 47.6 %collective-permute-start = (bf16[208,4096]{1,0:T(8,128)(2,1)S(1)}, bf16[208,4096]{1,0:T(8,128)(2,1)S(1)}, u32[]{:S(2)}, u32[]{:S(2)}) collective-permute-start(bf16[208,4096]{1,0:T(8,128)(2,1)S(1)} %fusion.1), channel_id=1, source_target_pairs={{0,16},{16,0},{1,17},{17,1},{2,18},{18,2},{3,19},{19,3},{4,20},{20... | collective-permute-start | bytes 5111816 | tf_op jit(solution)/shard_map/ppermute | solution.py:339
  51.6 1.2 %copy-start = (bf16[208,4096]{1,0:T(8,128)(2,1)}, bf16[208,4096]{1,0:T(8,128)(2,1)S(1)}, u32[]{:S(2)}) copy-start(bf16[208,4096]{1,0:T(8,128)(2,1)S(1)} %collective-permute-done) | copy-start | bytes 5111812
  51.6 7.1 %collective-permute-start.1 = (bf16[208,4096]{1,0:T(8,128)(2,1)S(1)}, bf16[208,4096]{1,0:T(8,128)(2,1)}, u32[]{:S(2)}, u32[]{:S(2)}) collective-permute-start(bf16[208,4096]{1,0:T(8,128)(2,1)S(1)} %collective-permute-done), channel_id=1, source_target_pairs={{0,1},{1,0},{2,3},{3,2},{4,5},{5,4},{6,7},{7,6},{8,9},{9,8},{10,11... | collective-permute-start | bytes 5111816 | tf_op jit(solution)/shard_map/ppermute | solution.py:346
  52.8 56.8 %all-to-all-start = ((bf16[16,208,256]{2,1,0:T(8,128)(2,1)}), bf16[16,208,256]{2,1,0:T(8,128)(2,1)S(1)}, u32[]{:S(2)}, u32[]{:S(2)}) async-start(bf16[16,208,256]{2,1,0:T(8,128)(2,1)} %get-tuple-element.18), calls=%async_computation | async-start | bytes 3407872 | tf_op jit(solution)/shard_map/all_to_all | solution.py:347
  58.8 51.0 %copy-start.2 = (s32[192,2]{0,1:T(2,128)S(1)}, s32[192,2]{0,1:T(2,128)}, u32[]{:S(2)}) copy-start(s32[192,2]{0,1:T(2,128)} %param.11) | copy-start | bytes 4612

commit v2 on v1

--- a/solution.py
+++ b/solution.py
@@ -41,6 +41,48 @@
 
 def in_place():
     return pl.BlockSpec(memory_space=pl.ANY)
+
+
+def my_place(shares):
+    index = lax.axis_index("dp")
+    return index // (shares // EXPERTS), index % 2, lax.axis_index("expert")
+
+
+def pack_body(shares, ids_ref, probs_ref, tok_hbm, out_hbm, routes_ref, send_hbm, tail_ref, sems):
+    _, parity, _ = my_place(shares)
+    count = tok_hbm.shape[0]
+    top = send_hbm.at[:count]
+
+    @pl.when(parity == 0)
+    def _():
+        pltpu.make_async_copy(tok_hbm, top, sems.at[0]).start()
+
+    @pl.when(parity == 1)
+    def _():
+        pltpu.make_async_copy(out_hbm, top, sems.at[0]).start()
+
+    ids = ids_ref[...].astype(F32)
+    routes = jnp.concatenate([ids, probs_ref[...].astype(F32), jnp.zeros((EXTRA - 4, count), F32)], axis=0).astype(BF)
+    routes_ref[...] = routes
+    tail_ref[...] = jnp.zeros_like(tail_ref)
+    tail_ref[:, :count] = routes
+    below = pltpu.make_async_copy(tail_ref, send_hbm.at[pl.ds(count, EXTRA)], sems.at[1])
+    below.start()
+    below.wait()
+    pltpu.make_async_copy(tok_hbm, top, sems.at[0]).wait()
+
+
+def pack(ids, probs, tokens, grad_out, shares):
+    count, width = tokens.shape
+    return pl.pallas_call(
+        functools.partial(pack_body, shares),
+        in_specs=[whole(ids.shape), whole(probs.shape), in_place(), in_place()],
+        out_specs=[whole((EXTRA, count)), in_place()],
+        out_shape=[jax.ShapeDtypeStruct((EXTRA, count), BF), jax.ShapeDtypeStruct((count + EXTRA, width), BF)],
+        scratch_shapes=[pltpu.VMEM((EXTRA, width), BF), pltpu.SemaphoreType.DMA((2,))],
+        cost_estimate=pl.CostEstimate(flops=0, bytes_accessed=4 * count * width, transcendentals=0),
+        name="pack",
+    )(ids, probs, tokens, grad_out)
 
 
 def slot_table(routes, owner, limit, backwards):
@@ -55,20 +97,19 @@
     rank = dot(wide, earlier)[:1].astype(jnp.int32)
     kept = (named > 0) & (rank < limit)
     slot = lax.broadcasted_iota(jnp.int32, (CAP, count), 0)
-    if backwards:
-        slot = CAP - 1 - slot
+    slot = jnp.where(backwards, CAP - 1 - slot, slot)
     table = ((slot == rank) & kept).astype(F32)
     return table, jnp.sum(table * weight, axis=1, keepdims=True)
 
 
 class Stream:
-    def __init__(self, sources, slots, sems, block):
+    def __init__(self, sources, slots, sems, block, steps):
         self.sources, self.slots, self.sems, self.block = sources, slots, sems, block
-        self.steps = sources[0].shape[1] // block
+        self.steps, self.whole = steps, sources[0].shape[1] == block
 
     def copy(self, i, step):
         source = self.sources[i]
-        if self.steps > 1:
+        if not self.whole:
             source = source.at[:, pl.ds(pl.multiple_of(step * self.block, self.block), self.block)]
         slot = lax.rem(step, 2)
         return pltpu.make_async_copy(source, self.slots[i].at[slot], self.sems.at[i, slot])
@@ -109,14 +150,15 @@
     return [(a, min(size, total - a)) for a in range(0, total, size)]
 
 
-def own_body(packed, place_ref, cap_ref, routes_ref, tok_hbm, out_hbm, wg_hbm, wu_hbm, wd_hbm,
-             dg_ref, du_ref, h_ref, part_ref, prob_ref, xq_ref, sq_ref, filled_ref,
-             tok_ref, out_ref, x_ref, u_ref, p_ref, table_ref, acc_ref, wg_ref, wu_ref, wd_ref, sems, row_sems):
+def own_body(packed, early, groups, cap_ref, routes_ref, tok_hbm, out_hbm, wg_hbm, wu_hbm, wd_hbm, *refs):
+    acts_refs, refs = (refs[:3], refs[3:]) if early is None else (refs[:4], refs[4:])
+    (part_ref, prob_ref, xq_ref, sq_ref, filled_ref, tok_ref, out_ref, x_ref, u_ref, p_ref, table_ref, acc_ref,
+     wg_ref, wu_ref, wd_ref, sems, row_sems) = refs
     step = pl.program_id(0)
     width, block = wg_ref.shape[1:]
     quarter = xq_ref.shape[1]
-    stream = Stream((wg_hbm, wu_hbm, wd_hbm), (wg_ref, wu_ref, wd_ref), sems, block)
-    owner, group = place_ref[0], place_ref[2]
+    stream = Stream((wg_hbm, wu_hbm, wd_hbm), (wg_ref, wu_ref, wd_ref), sems, block, wg_hbm.shape[1] // block)
+    owner, _, group = my_place(part_ref.shape[0])
 
     @pl.when(step == 0)
     def _():
@@ -125,7 +167,7 @@
         for copy in rows:
             copy.start()
         stream.first()
-        table, p = slot_table(routes_ref[...].astype(F32), owner, cap_ref[owner], False)
+        table, p = slot_table(routes_ref[...].astype(F32), owner, cap_ref[owner], (group == 1) & (groups == 2))
         table_ref[...] = table.astype(BF)
         p_ref[...] = p
         filled_ref[...] = jnp.sum(table, axis=1, keepdims=True)
@@ -141,9 +183,22 @@
 
     stream.ahead(step)
     d_gate, d_up, hidden, back, wg, wu = derivatives(x_ref, u_ref, p_ref[...], stream, step)
-    dg_ref[...] = d_gate
-    du_ref[...] = d_up
-    h_ref[...] = hidden
+    acts = (d_gate, d_up, hidden)
+
+    def store_early():
+        for ref, value in zip(acts_refs, acts):
+            ref[...] = value
+
+    if early is None:
+        store_early()
+    else:
+        pl.when(step < early)(store_early)
+
+        @pl.when(step >= early)
+        def _():
+            for i, value in enumerate(acts):
+                acts_refs[3][i] = value
+
     prob_ref[...] += jnp.sum(hidden.astype(F32) * back, axis=1, keepdims=True)
     gate_t = d_gate.T
     up_t = d_up.T
@@ -174,52 +229,73 @@
     return [pltpu.VMEM((2, width, block), BF)] * 3 + [pltpu.SemaphoreType.DMA((3, 2))]
 
 
-def own_group(place, capacity, routes, tokens, grad_out, wg, wu, wd, shares, groups, packed, block):
+def own_group(capacity, routes, tokens, grad_out, wg, wu, wd, shares, groups, packed, block, early):
     count, width = tokens.shape
     hidden = wg.shape[1]
+    steps = hidden // block
     tall = count + (EXTRA if packed else 0)
     fw = width // shares
     quarter = width // groups
-    act = pl.BlockSpec((CAP, block), lambda j: (0, j))
-    acts = jax.ShapeDtypeStruct((CAP, hidden), BF)
+    act_specs = [pl.BlockSpec((CAP, block), lambda j: (0, jnp.minimum(j, early - 1)))] * 3
+    acts = [jax.ShapeDtypeStruct((CAP, early * block), BF)] * 3
+    if early < steps:
+        act_specs.append(pl.BlockSpec((3, CAP, block), lambda j: (0, 0, jnp.maximum(j - early, 0))))
+        acts.append(jax.ShapeDtypeStruct((3, CAP, (steps - early) * block), BF))
     column = jax.ShapeDtypeStruct((CAP, 1), F32)
     share = jax.ShapeDtypeStruct((CAP, quarter), BF)
     part = jax.ShapeDtypeStruct((shares, tall, fw), BF)
     rows = pltpu.VMEM((CAP, width), BF)
     tall_rows = pltpu.VMEM((count, width), BF)
     return pl.pallas_call(
-        functools.partial(own_body, packed),
-        grid=(hidden // block,),
-        in_specs=[whole_smem(), whole_smem(), whole(routes.shape)] + [in_place()] * 5,
-        out_specs=[act, act, act, whole(part.shape), whole(column.shape), whole(share.shape), whole(share.shape),
-                   whole(column.shape)],
-        out_shape=[acts, acts, acts, part, column, share, share, column],
+        functools.partial(own_body, packed, early if early < steps else None, groups),
+        grid=(steps,),
+        in_specs=[whole_smem(), whole(routes.shape)] + [in_place()] * 5,
+        out_specs=act_specs + [whole(part.shape), whole(column.shape), whole(share.shape), whole(share.shape),
+                               whole(column.shape)],
+        out_shape=acts + [part, column, share, share, column],
         scratch_shapes=[tall_rows, tall_rows, rows, rows, pltpu.VMEM((CAP, 1), F32), pltpu.VMEM((CAP, count), BF),
                         pltpu.VMEM((width, CAP), F32)] + weight_slots(width, block) + [pltpu.SemaphoreType.DMA((2,))],
         compiler_params=params(),
         cost_estimate=pl.CostEstimate(
             flops=10 * CAP * width * hidden, bytes_accessed=6 * width * hidden, transcendentals=CAP * hidden),
         name="own_group",
-    )(place, capacity, routes, tokens, grad_out, wg, wu, wd)
-
-
-def weights_body(groups, place_ref, cap_ref, xq_ref, sq_ref, filled_ref, one_hbm, two_hbm, dg_ref, du_ref, h_ref,
-                 wg_hbm, wu_hbm, wd_hbm, gg_ref, gu_ref, gd_ref,
-                 one_ref, two_ref, xo_ref, uo_ref, po_ref, xs_ref, ss_ref, short_ref, wg_ref, wu_ref, wd_ref, sems, row_sems):
-    step = pl.program_id(0)
-    owner, parity, group = place_ref[0], place_ref[1], place_ref[2]
-    quarter = xs_ref.shape[1]
-    others = xo_ref.shape[0]
-    count = one_ref.shape[1] - EXTRA
+    )(capacity, routes, tokens, grad_out, wg, wu, wd)
+
+
+def joined(mine, other):
+    return jnp.concatenate([mine, other], axis=0)
+
+
+def merged(group, mine, other):
+    first, last = jnp.where(group == 0, mine, other), jnp.where(group == 0, other, mine)
     lead = SHORT - CAP
     shared = CAP - lead
-    stream = Stream((wg_hbm, wu_hbm, wd_hbm), (wg_ref, wu_ref, wd_ref), sems, wg_ref.shape[2])
-
-    def joined(mine, other):
-        return jnp.concatenate([mine, other], axis=0)
-
-    def merged(mine, other):
-        return jnp.concatenate([mine[:lead], mine[lead:] + other[:shared], other[shared:]], axis=0)
+    return jnp.concatenate([first[:lead], first[lead:] + last[:shared], last[shared:]], axis=0)
+
+
+def store_grads(groups, group, fits_ref, xs_ref, ss_ref, mine, other, out_refs):
+    def grads(join, rows):
+        for i, (rows_ref, out_ref) in enumerate(zip((xs_ref, xs_ref, ss_ref), out_refs)):
+            out_ref[...] = dotg(rows_ref[:rows, :], join(mine(i), other(i)), FIRST).astype(BF)
+
+    if groups == 2:
+        @pl.when(fits_ref[0] == 1)
+        def _():
+            grads(functools.partial(merged, group), SHORT)
+
+    @pl.when(fits_ref[0] == 0)
+    def _():
+        grads(joined, xs_ref.shape[0])
+
+
+def again_body(groups, shares, steps, cap_ref, xq_ref, sq_ref, filled_ref, one_hbm, two_hbm, dg_ref, du_ref, h_ref,
+               wg_hbm, wu_hbm, wd_hbm, gg_ref, gu_ref, gd_ref, xs_ref, ss_ref, fits_ref,
+               one_ref, two_ref, xo_ref, uo_ref, po_ref, wg_ref, wu_ref, wd_ref, sems, row_sems):
+    step = pl.program_id(0)
+    owner, parity, group = my_place(shares)
+    quarter = xs_ref.shape[1]
+    count = one_ref.shape[1] - EXTRA
+    stream = Stream((wg_hbm, wu_hbm, wd_hbm), (wg_ref, wu_ref, wd_ref), sems, wg_ref.shape[2], steps)
 
     @pl.when(step == 0)
     def _():
@@ -234,7 +310,7 @@
         for g in range(groups - 1):
             at = slice(g * CAP, (g + 1) * CAP)
             routes = one_ref[g, count:count + 8, :count].astype(F32)
-            table, p = slot_table(routes, owner, cap_ref[owner], groups == 2)
+            table, p = slot_table(routes, owner, cap_ref[owner], (group == 0) & (groups == 2))
             filled += jnp.sum(table)
             po_ref[at, :] = p
             table = table.astype(BF)
@@ -252,7 +328,7 @@
                 uo_ref[at, :] = from_one
 
         fits = filled <= SHORT if groups == 2 else jnp.bool_(False)
-        short_ref[0] = fits.astype(jnp.int32)
+        fits_ref[0] = fits.astype(jnp.int32)
         part = pl.ds(pl.multiple_of(group * quarter, quarter), quarter)
         mine, scaled = xq_ref[...], sq_ref[...]
         other = xo_ref[:, part]
@@ -260,8 +336,8 @@
         if groups == 2:
             @pl.when(fits)
             def _():
-                xs_ref[:SHORT, :] = merged(mine, other)
-                ss_ref[:SHORT, :] = merged(scaled, scaled_other)
+                xs_ref[:SHORT, :] = merged(group, mine, other)
+                ss_ref[:SHORT, :] = merged(group, scaled, scaled_other)
 
         @pl.when(jnp.logical_not(fits))
         def _():
@@ -269,48 +345,61 @@
             ss_ref[...] = joined(scaled, scaled_other)
 
     stream.ahead(step)
-    d_gate, d_up, hidden, _, _, _ = derivatives(xo_ref, uo_ref, po_ref[...], stream, step)
-
-    def grads(join, rows):
-        xs = xs_ref[:rows, :]
-        gg_ref[...] = dotg(xs, join(dg_ref[...], d_gate), FIRST).astype(BF)
-        gu_ref[...] = dotg(xs, join(du_ref[...], d_up), FIRST).astype(BF)
-        gd_ref[...] = dotg(ss_ref[:rows, :], join(h_ref[...], hidden), FIRST).astype(BF)
-
-    if groups == 2:
-        @pl.when(short_ref[0] == 1)
-        def _():
-            grads(merged, SHORT)
-
-    @pl.when(short_ref[0] == 0)
-    def _():
-        grads(joined, CAP + others)
-
-
-def weight_grads(place, capacity, xq, sq, filled, one, two, dg, du, h, wg, wu, wd, groups, block):
+    acts = derivatives(xo_ref, uo_ref, po_ref[...], stream, step)
+    own = (dg_ref, du_ref, h_ref)
+    store_grads(groups, group, fits_ref, xs_ref, ss_ref, lambda i: own[i][...], lambda i: acts[i], (gg_ref, gu_ref, gd_ref))
+
+
+def grads_again(capacity, xq, sq, filled, one, two, dg, du, h, wg, wu, wd, groups, shares, block):
     width, hidden = wg.shape
     others = (groups - 1) * CAP
     quarter = width // groups
+    steps = dg.shape[1] // block
     act = pl.BlockSpec((CAP, block), lambda j: (0, j))
     grad = pl.BlockSpec((quarter, block), lambda j: (0, j))
     arrived = pltpu.VMEM(one.shape, BF)
     rows = pltpu.VMEM((others, width), BF)
-    share = pltpu.VMEM((CAP + others, quarter), BF)
+    joint = jax.ShapeDtypeStruct((CAP + others, quarter), BF)
     return pl.pallas_call(
-        functools.partial(weights_body, groups),
-        grid=(hidden // block,),
-        in_specs=[whole_smem(), whole_smem(), whole(xq.shape), whole(sq.shape), whole(filled.shape), in_place(), in_place(),
+        functools.partial(again_body, groups, shares, steps),
+        grid=(steps,),
+        in_specs=[whole_smem(), whole(xq.shape), whole(sq.shape), whole(filled.shape), in_place(), in_place(),
                   act, act, act, in_place(), in_place(), in_place()],
+        out_specs=[grad] * 3 + [whole(joint.shape)] * 2 + [whole_smem()],
+        out_shape=[jax.ShapeDtypeStruct((quarter, hidden), BF)] * 3 + [joint] * 2 + [jax.ShapeDtypeStruct((1,), jnp.int32)],
+        scratch_shapes=[arrived, arrived, rows, rows, pltpu.VMEM((others, 1), F32)]
+        + weight_slots(width, block) + [pltpu.SemaphoreType.DMA((2,))],
+        compiler_params=params(),
+        cost_estimate=pl.CostEstimate(
+            flops=(6 * others * width + 6 * (CAP + others) * quarter) * steps * block,
+            bytes_accessed=6 * (width + quarter) * steps * block, transcendentals=others * steps * block),
+        name="grads_again",
+    )(capacity, xq, sq, filled, one, two, dg, du, h, wg, wu, wd)
+
+
+def given_body(groups, shares, fits_ref, xs_ref, ss_ref, mine_ref, other_ref, gg_in, gu_in, gd_in, gg_ref, gu_ref, gd_ref):
+    _, _, group = my_place(shares)
+    store_grads(groups, group, fits_ref, xs_ref, ss_ref, lambda i: mine_ref[i], lambda i: other_ref[i], (gg_ref, gu_ref, gd_ref))
+
+
+def grads_given(fits, xs, ss, mine, other, grads, groups, shares, block):
+    quarter, hidden = grads[0].shape
+    steps = mine.shape[2] // block
+    early = hidden // block - steps
+    act = pl.BlockSpec((3, CAP, block), lambda j: (0, 0, j))
+    grad = pl.BlockSpec((quarter, block), lambda j: (0, j + early))
+    return pl.pallas_call(
+        functools.partial(given_body, groups, shares),
+        grid=(steps,),
+        in_specs=[whole_smem(), whole(xs.shape), whole(ss.shape), act, act] + [in_place()] * 3,
         out_specs=[grad] * 3,
         out_shape=[jax.ShapeDtypeStruct((quarter, hidden), BF)] * 3,
-        scratch_shapes=[arrived, arrived, rows, rows, pltpu.VMEM((others, 1), F32), share, share,
-                        pltpu.SMEM((1,), jnp.int32)] + weight_slots(width, block) + [pltpu.SemaphoreType.DMA((2,))],
+        input_output_aliases={5: 0, 6: 1, 7: 2},
         compiler_params=params(),
         cost_estimate=pl.CostEstimate(
-            flops=6 * others * width * hidden + 6 * (CAP + others) * quarter * hidden,
-            bytes_accessed=6 * width * hidden + 6 * quarter * hidden, transcendentals=others * hidden),
-        name="weight_grads",
-    )(place, capacity, xq, sq, filled, one, two, dg, du, h, wg, wu, wd)
+            flops=6 * xs.shape[0] * quarter * steps * block, bytes_accessed=6 * quarter * steps * block, transcendentals=0),
+        name="grads_given",
+    )(fits, xs, ss, mine, other, *grads)
 
 
 def block_of(hidden, largest):
@@ -326,39 +415,42 @@
     count, width = tokens.shape
     hidden = w_gate.shape[1]
     per_expert = shares // EXPERTS
-    index = lax.axis_index("dp")
-    owner = index // per_expert
-    parity = index % 2
-    place = jnp.stack([owner, parity, lax.axis_index("expert")]).astype(jnp.int32)
     packed = width // shares >= count
-
-    routes = jnp.concatenate([expert_ids.T.astype(BF), gate_probs.T, jnp.zeros((EXTRA - 4, count), BF)], axis=0)
-    send = jnp.concatenate(
-        [jnp.where(parity == 0, tokens, grad_out), jnp.pad(routes, ((0, 0), (0, width - count)))], axis=0)
+    block = block_of(hidden, 512)
+    steps = hidden // block
+    early = steps - steps * 3 // 7 if groups == 2 else steps
+
+    routes, send = pack(expert_ids.T, gate_probs.T, tokens, grad_out, shares)
     arounds = [[(i, (i + shift) % groups) for i in range(groups)] for shift in range(1, groups)]
     one = [lax.ppermute(send, "expert", around) for around in arounds]
 
-    dg, du, h, part, prob, xq, sq, filled = own_group(
-        place, capacity, routes, tokens, grad_out, w_gate, w_up, w_down, shares, groups, packed, block_of(hidden, 512))
+    *acts, part, prob, xq, sq, filled = own_group(
+        capacity, routes, tokens, grad_out, w_gate, w_up, w_down, shares, groups, packed, block, early)
 
     one, part = lax.optimization_barrier((one, part))
     swap = [(i, i ^ 1) for i in range(shares)]
     two = [lax.ppermute(rows, "dp", swap) for rows in one]
+    if early < steps:
+        late = acts.pop()
+        late_other = lax.ppermute(late, "expert", arounds[0])
     arrived = lax.all_to_all(part, "dp", split_axis=0, concat_axis=0, tiled=True)
 
     def stacked(parts):
         return parts[0][None] if len(parts) == 1 else jnp.stack(parts)
 
-    grad_gate, grad_up, grad_down = weight_grads(
-        place, capacity, xq, sq, filled, stacked(one), stacked(two), dg, du, h, w_gate, w_up, w_down, groups,
-        block_of(hidden, 512))
+    *grads, xs, ss, fits = grads_again(
+        capacity, xq, sq, filled, stacked(one), stacked(two), *acts, w_gate, w_up, w_down, groups, shares, block)
+    if early < steps:
+        grads = grads_given(fits, xs, ss, late, late_other, grads, groups, shares, block)
+    grad_gate, grad_up, grad_down = grads
 
     token_grad = jnp.sum(arrived[:, :count].astype(F32), axis=0).astype(BF)
     if packed:
         ends = arrived[:, count:count + 2, :count].astype(F32)
         by_expert = jnp.sum(ends.reshape(EXPERTS, per_expert * 2, count), axis=1)
     else:
-        table, _ = slot_table(routes.astype(F32), owner, capacity[owner], False)
+        owner, _, group = my_place(shares)
+        table, _ = slot_table(routes.astype(F32), owner, capacity[owner], (group == 1) & (groups == 2))
         mine = jnp.sum(table * prob, axis=0)
         one_hot = (jnp.arange(EXPERTS) == owner).astype(F32)
         by_expert = lax.psum(one_hot[:, None] * mine[None, :], "dp")

time: 112 us -> 150 us (1.34)
  Pallas kernels: 94.8 us -> 137 us
  other arithmetic: 5.41 us -> 1.51 us
    pallas_call x2 -> x4, Pallas kernels: 94.8 us -> 137 us  [the longest x1 50.1 us: pack(): pl.pallas_call(functools.partial(pack_body, shares), in_specs=[whole(ids....]
    select_n x1 -> x0, other arithmetic: 1.58 us -> none  [per_device(): jnp.where(parity == 0, tokens, grad_out)]
  transfers between devices with their start and end apart: 3 -> 4, of which waited for: 0 -> 0; matrix products, arithmetic and copies ran while one was open for 1% -> 0% of each run, Pallas kernels for 85% -> 58%
where the time goes in v2:
time: 150 us
  Pallas kernels  137 us (91%)
  starting transfers between devices  9.63 us (6%)
  other arithmetic  1.51 us (1%)
    pallas_call x1, Pallas kernels, pack(): pl.pallas_call(functools.partial(pack_body, shares), in_specs=[whole(ids....  50.1 us
    pallas_call x1, Pallas kernels, own_group(): pl.pallas_call(functools.partial(own_body, packed, early if early < steps...  43.3 us
    pallas_call x1, Pallas kernels, grads_again(): pl.pallas_call(functools.partial(again_body, groups, shares, steps), grid...  32 us
    pallas_call x1, Pallas kernels, grads_given(): pl.pallas_call(functools.partial(given_body, groups, shares), grid=(steps...  11.8 us
    all_to_all x1, starting transfers between devices, per_device(): lax.all_to_all(part, 'dp', split_axis=0, concat_axis=0, tiled=True)  5.96 us
    ppermute x1, starting transfers between devices, per_device(): one = [lax.ppermute(send, 'expert', around) for around in arounds]  3 us
  transfers between devices with their start and end apart: 4, of which 0 were waited for; matrix products, arithmetic and copies ran while one was open for 0% of the time, Pallas kernels for 58%

profile of v2, /device:TPU:0, one launch (start us, length us, event | category | flops | bytes accessed | tf_op | source)
XLA Modules:
  0.0 150.1 jit_solution(5003517722427553071)
XLA Ops:
  0.6 50.1 %pack.1 = (bf16[16,192]{1,0:T(8,128)(2,1)}, bf16[208,4096]{1,0:T(8,128)(2,1)}) custom-call(s32[2,192]{1,0:T(2,128)} %bitcast.7, bf16[2,192]{1,0:T(2,128)(2,1)} %bitcast.8, bf16[192,4096]{1,0:T(8,128)(2,1)} %tok_hbm.3, bf16[192,4096]{1,0:T(8,128)(2,1)} %out_hbm.3), custom_call_target="tpu_custom_call" | custom-call | bytes 3145728 | tf_op jit(solution)/shard_map/pack/pallas_call | solution.py:77
  50.7 3.0 %collective-permute-start = (bf16[208,4096]{1,0:T(8,128)(2,1)}, bf16[208,4096]{1,0:T(8,128)(2,1)S(1)}, u32[]{:S(2)}, u32[]{:S(2)}) collective-permute-start(bf16[208,4096]{1,0:T(8,128)(2,1)} %get-tuple-element.26), channel_id=1, source_target_pairs={{0,16},{16,0},{1,17},{17,1},{2,18},{18,2},{3,19},{19,3},{4,20},{20... | collective-permute-start | bytes 5111816 | tf_op jit(solution)/shard_map/ppermute | solution.py:425
  53.7 43.3 %own_group.1 = (bf16[144,2048]{1,0:T(8,128)(2,1)}, bf16[144,2048]{1,0:T(8,128)(2,1)}, bf16[144,2048]{1,0:T(8,128)(2,1)}, bf16[3,144,1536]{2,1,0:T(8,128)(2,1)}, ...) custom-call(s32[4]{0:T(128)} %cap_ref.3, ...), custom_call_target="tpu_custom_call" | custom-call | flops 21139292160 | bytes 88080384 | tf_op jit(solution)/shard_map/own_group/pallas_call | solution.py:249
  97.0 0.0 collective-permute-done
  97.0 0.0 copy-start
  97.0 0.1 collective-permute-start.1
  97.1 1.1 copy-done
  98.2 6.0 %all-to-all-start = ((bf16[16,208,256]{2,1,0:T(8,128)(2,1)}), bf16[16,208,256]{2,1,0:T(8,128)(2,1)S(1)}, u32[]{:S(2)}, u32[]{:S(2)}) async-start(bf16[16,208,256]{2,1,0:T(8,128)(2,1)} %get-tuple-element.29), calls=%async_computation | async-start | bytes 3407872 | tf_op jit(solution)/shard_map/all_to_all | solution.py:436
  104.1 0.6 collective-permute-start.2
  104.7 0.0 collective-permute-done.1
  104.7 32.0 %grads_again.1 = (bf16[2048,3584]{1,0:T(8,128)(2,1)}, bf16[2048,3584]{1,0:T(8,128)(2,1)}, bf16[2048,3584]{1,0:T(8,128)(2,1)}, bf16[288,2048]{1,0:T(8,128)(2,1)}, bf16[288,2048]{1,0:T(8,128)(2,1)}, /*index=5*/s32[1]{0:T(128)}) custom-call(s32[4]{0:T(128)} %cap_ref.3, bf16[144,2048]{1,0:T(8,128)(2,1)} %get-tuple-element.30.xq_ref, ...), custom_call_target="tpu_custom_call" | custom-call | flops 14495514624 | bytes 75497472 | tf_op jit(solution)/shard_map/grads_again/pallas_call | solution.py:363
  136.7 0.0 collective-permute-done.2.other_ref
  136.8 0.0 copy-start.1
  136.8 11.8 %grads_given.1 = (bf16[2048,3584]{1,0:T(8,128)(2,1)}, bf16[2048,3584]{1,0:T(8,128)(2,1)}, bf16[2048,3584]{1,0:T(8,128)(2,1)}) custom-call(s32[1]{0:T(128)} %get-tuple-element.37.fits_ref, bf16[288,2048]{1,0:T(8,128)(2,1)} %get-tuple-element.38.xs_ref, ...), custom_call_target="tpu_custom_call", output_to_operand_aliasing={{0}: (5, {}), {1}: (6, {}), {2}: (7, {})} | custom-call | flops 5435817984 | bytes 18874368 | tf_op jit(solution)/shard_map/grads_given/pallas_call | solution.py:391
  148.6 0.0 all-to-all-done
  148.7 0.0 copy-done.1
  148.7 0.6 select_reduce_fusion
  149.2 0.9 slice_reduce_fusion
  (3 shorter events, 0.1 us)
Async XLA Ops:
  50.7 46.3 %collective-permute-start = (bf16[208,4096]{1,0:T(8,128)(2,1)}, bf16[208,4096]{1,0:T(8,128)(2,1)S(1)}, u32[]{:S(2)}, u32[]{:S(2)}) collective-permute-start(bf16[208,4096]{1,0:T(8,128)(2,1)} %get-tuple-element.26), channel_id=1, source_target_pairs={{0,16},{16,0},{1,17},{17,1},{2,18},{18,2},{3,19},{19,3},{4,20},{20... | collective-permute-start | bytes 5111816 | tf_op jit(solution)/shard_map/ppermute | solution.py:425
  97.0 1.2 copy-start
  97.0 7.7 %collective-permute-start.1 = (bf16[208,4096]{1,0:T(8,128)(2,1)S(1)}, bf16[208,4096]{1,0:T(8,128)(2,1)}, u32[]{:S(2)}, u32[]{:S(2)}) collective-permute-start(bf16[208,4096]{1,0:T(8,128)(2,1)S(1)} %collective-permute-done), channel_id=1, source_target_pairs={{0,1},{1,0},{2,3},{3,2},{4,5},{5,4},{6,7},{7,6},{8,9},{9,8},{10,11... | collective-permute-start | bytes 5111816 | tf_op jit(solution)/shard_map/ppermute | solution.py:432
  98.2 50.4 %all-to-all-start = ((bf16[16,208,256]{2,1,0:T(8,128)(2,1)}), bf16[16,208,256]{2,1,0:T(8,128)(2,1)S(1)}, u32[]{:S(2)}, u32[]{:S(2)}) async-start(bf16[16,208,256]{2,1,0:T(8,128)(2,1)} %get-tuple-element.29), calls=%async_computation | async-start | bytes 3407872 | tf_op jit(solution)/shard_map/all_to_all | solution.py:436
  104.1 32.6 %collective-permute-start.2 = (bf16[3,144,1536]{2,1,0:T(8,128)(2,1)}, bf16[3,144,1536]{2,1,0:T(8,128)(2,1)}, u32[]{:S(2)}, u32[]{:S(2)}) collective-permute-start(bf16[3,144,1536]{2,1,0:T(8,128)(2,1)} %get-tuple-element.40.mine_ref), channel_id=1, source_target_pairs={{0,16},{16,0},{1,17},{17,1},{2,18},{18,2},{3,19},{19,3},{4,20},{20... | collective-permute-start | bytes 3981320 | tf_op jit(solution)/shard_map/ppermute | solution.py:435
  136.8 11.9 %copy-start.1 = (s32[192,2]{0,1:T(2,128)S(1)}, s32[192,2]{0,1:T(2,128)}, u32[]{:S(2)}) copy-start(s32[192,2]{0,1:T(2,128)} %param.11) | copy-start | bytes 4612
